TPU v7x, 128 devices: a whole 4x4x4 slice. The times are simulated.
128 devices in a mesh: gx: 8 (over x_hi, y), gy: 16 (over z, x_lo, core).
Axes of the slice: x: 4 (x_hi: 2, x_lo: 2; x = x_hi * 2 + x_lo), y: 4, z: 4, core: 2. Of those that a mesh axis runs over, the one named last changes fastest.
Arguments:
- charges: bfloat16 [32, 64, 16, 256], P('gx', 'gy'), may hold values from -6 to 6
- basis: bfloat16 [32, 64, 64, 256], P('gx', 'gy'), may hold values from -0.375 to 0.375
- near_blocks: bfloat16 [32, 64, 8, 256, 256], P('gx', 'gy'), may hold values from -0.125 to 0.125
- near_list: int32 [32, 64, 8], P('gx', 'gy'), may hold values from 0 to 8, as said below
- far_list: int32 [32, 64, 8], P('gx', 'gy'), may hold values from 0 to 15, as said below
- coupling: bfloat16 [32, 64, 64, 512], P('gx', 'gy'), may hold values from -0.25 to 0.25
- transfer: bfloat16 [32, 64, 64, 64], P('gx', 'gy'), may hold values from -0.375 to 0.375
- coarse_transfer: bfloat16 [8, 16, 64, 64], P('gx', 'gy'), may hold values from -0.375 to 0.375
- coarse_group: int32 [128], replicated, may hold values from 0 to 15, as said below
- coarse_pattern: int32 [16, 16], replicated, may hold values 0 or 1
- coarse_coupling: bfloat16 [16, 64, 1024], replicated, may hold values from -0.1875 to 0.1875
Outputs:
- potential: bfloat16 [32, 64, 16, 256], P('gx', 'gy')
Inputs may be any that keep to these rules, and one draw needn't show every extreme that they name: `near_list`: the 8 entries of one leaf are distinct. `far_list`: the 8 entries of one leaf are distinct. `coarse_group`: every coarse cluster has exactly 8 device clusters.
All inputs are finite; a program needn't handle non-finite values.
Results may differ from a plain program's by a relative error of at most 0.015.
Values may be sent and summed in bfloat16 or wider, within the bound.
A program may use at most 64 MiB of HBM per device.

v0:
```python
import jax
import jax.numpy as jnp
from jax import lax
from jax.sharding import PartitionSpec as P

GROUP = 8


cycle_offsets = [
    (shift_x, shift_y)
    for shift_x in range(-2, 3)
    for shift_y in range(-2, 3)
    if max(abs(shift_x), abs(shift_y)) == 2
]
near_offsets = [(number // 3 - 1, number % 3 - 1) for number in range(9)]


def with_halo(cells, sides, width):
    for axis, dim in sides:
        count = lax.axis_size(axis)
        head = lax.slice_in_dim(cells, 0, width, axis=dim)
        tail = lax.slice_in_dim(cells, cells.shape[dim] - width, cells.shape[dim], axis=dim)
        cells = jnp.concatenate(
            [
                lax.ppermute(tail, axis, [(i, (i + 1) % count) for i in range(count)]),
                cells,
                lax.ppermute(head, axis, [((i + 1) % count, i) for i in range(count)]),
            ],
            axis=dim,
        )
    return cells


def shifted_stack(padded, margin, offsets, leaves_x, leaves_y):
    pieces = [
        padded[
            margin + shift_x : margin + shift_x + leaves_x,
            margin + shift_y : margin + shift_y + leaves_y,
        ]
        for shift_x, shift_y in offsets
    ]
    stacked = jnp.stack(pieces)
    return stacked.reshape(stacked.shape[0], leaves_x, leaves_y, -1)


def pick_rows(stacked, wanted):
    options = lax.broadcasted_iota(jnp.int32, (stacked.shape[0],), 0)
    one_hot = (wanted[:, :, :, None] == options).astype(jnp.bfloat16)
    return jnp.einsum(
        "xysr,rxyz->xysz", one_hot, stacked, preferred_element_type=jnp.float32
    ).astype(jnp.bfloat16)


def coarse_product(coarse_coupling, coarse_pattern, coarse_coef, my_group):
    basis_rank = coarse_coef.shape[1]
    row_weights = lax.dynamic_index_in_dim(coarse_coupling, my_group, 0, keepdims=False)
    row_mask = lax.dynamic_index_in_dim(coarse_pattern, my_group, 0, keepdims=False)
    column_mask = jnp.repeat(row_mask, basis_rank).astype(jnp.bfloat16)
    masked = row_weights * column_mask[None, :]
    return jnp.dot(
        masked, coarse_coef.reshape(-1, coarse_coef.shape[2]), preferred_element_type=jnp.float32
    )


def local(
    charges,
    basis,
    near_blocks,
    near_list,
    far_list,
    coupling,
    transfer,
    coarse_transfer,
    coarse_group,
    coarse_pattern,
    coarse_coupling,
):
    leaves_x, leaves_y = (charges.shape[0], charges.shape[1])
    vectors, points = (charges.shape[2], charges.shape[3])
    basis_rank = basis.shape[2]
    padded_charges = with_halo(charges, (("gx", 0), ("gy", 1)), 1)
    leaf_coef = jnp.einsum(
        "abkp,abvp->abkv", basis, charges, preferred_element_type=jnp.float32
    ).astype(jnp.bfloat16)
    padded_coef = with_halo(leaf_coef, (("gx", 0), ("gy", 1)), 2)
    cluster_coef = jnp.einsum(
        "abkl,ablv->kv", transfer, leaf_coef, preferred_element_type=jnp.float32
    ).astype(jnp.bfloat16)
    own_transfer = coarse_transfer[0, 0]
    coarse_term = jnp.dot(own_transfer, cluster_coef, preferred_element_type=jnp.float32)
    cluster_count = lax.axis_size("gx") * lax.axis_size("gy")
    group_count = cluster_count // GROUP
    own_index = lax.axis_index("gx") * lax.axis_size("gy") + lax.axis_index("gy")
    my_group = coarse_group[own_index]
    group_index = lax.broadcasted_iota(jnp.int32, (group_count,), 0)
    placed = jnp.where((group_index == my_group)[:, None, None], coarse_term[None], 0.0)
    coarse_sum = lax.psum(placed, ("gx", "gy"))
    coarse_coef = coarse_sum.astype(jnp.bfloat16)
    group_far = coarse_product(coarse_coupling, coarse_pattern, coarse_coef, my_group).astype(
        jnp.bfloat16
    )
    cluster_far = jnp.einsum(
        "lk,lv->kv", own_transfer, group_far, preferred_element_type=jnp.float32
    ).astype(jnp.bfloat16)
    lowered = jnp.einsum("ablk,lv->abkv", transfer, cluster_far, preferred_element_type=jnp.float32)
    cycle_coef = shifted_stack(padded_coef, 2, cycle_offsets, leaves_x, leaves_y)
    far_count = far_list.shape[2]
    far_coef = pick_rows(cycle_coef, far_list).reshape(
        leaves_x, leaves_y, far_count * basis_rank, vectors
    )
    coupled = jnp.einsum("abkc,abcv->abkv", coupling, far_coef, preferred_element_type=jnp.float32)
    leaf_far = (coupled + lowered).astype(jnp.bfloat16)
    far_part = jnp.einsum("abkp,abkv->abvp", basis, leaf_far, preferred_element_type=jnp.float32)
    near_stack = shifted_stack(padded_charges, 1, near_offsets, leaves_x, leaves_y)
    near_count = near_list.shape[2]
    near_charges = pick_rows(near_stack, near_list).reshape(
        leaves_x, leaves_y, near_count, vectors, points
    )
    near_part = jnp.einsum(
        "abmpq,abmvq->abvp", near_blocks, near_charges, preferred_element_type=jnp.float32
    )
    return (far_part + near_part).astype(jnp.bfloat16)


def solution(mesh):
    return jax.shard_map(
        local,
        mesh=mesh,
        in_specs=(
            P("gx", "gy", None, None),
            P("gx", "gy", None, None),
            P("gx", "gy", None, None, None),
            P("gx", "gy", None),
            P("gx", "gy", None),
            P("gx", "gy", None, None),
            P("gx", "gy", None, None),
            P("gx", "gy", None, None),
            P(),
            P(),
            P(),
        ),
        out_specs=P("gx", "gy", None, None),
        check_vma=False,
    )
```

profile of v0, /device:TPU:1, one launch (start us, length us, event | category | flops | bytes accessed | tf_op | source)
XLA Modules:
  0.0 149.8 jit_solution(15131845637070346717)
XLA Ops:
  0.0 0.9 fusion.30
  0.9 6.0 %collective-permute-start.5 = (bf16[1,4,16,256]{3,2,1,0:T(8,128)(2,1)S(1)}, bf16[1,4,16,256]{3,2,1,0:T(8,128)(2,1)S(1)}, u32[]{:S(2)}, u32[]{:S(2)}) collective-permute-start(bf16[1,4,16,256]{3,2,1,0:T(8,128)(2,1)S(1)} %get-tuple-element.37), channel_id=1, source_target_pairs={{16,0},{32,16},{48,32},{64,48},{80,64},{96,80},{112,96},{0,112},{1... | collective-permute-start | bytes 98312 | tf_op jit(solution)/shard_map/ppermute | solution.py:27
  6.9 1.3 convolution_convert_fusion.2
  8.3 5.1 %collective-permute-start.1 = (bf16[2,4,64,16]{2,3,1,0:T(8,128)(2,1)S(1)}, bf16[2,4,64,16]{2,3,1,0:T(8,128)(2,1)S(1)}, u32[]{:S(2)}, u32[]{:S(2)}) collective-permute-start(bf16[2,4,64,16]{2,3,1,0:T(8,128)(2,1)S(1)} %get-tuple-element.42), channel_id=1, source_target_pairs={{16,0},{32,16},{48,32},{64,48},{80,64},{96,80},{112,96},{0,112},{1... | collective-permute-start | bytes 49160 | tf_op jit(solution)/shard_map/ppermute | solution.py:27
  13.4 1.2 dynamic_slice.11
  14.7 0.6 iota_compare_fusion.4
  16.6 1.2 convolution_bitcast_fusion.3
  18.1 71.5 %psum.7 = bf16[16,64,16]{2,1,0:T(8,128)(2,1)S(1)} all-reduce(f32[16,64,16]{2,1,0:T(8,128)S(1)} %broadcast_select_fusion), channel_id=1, replica_groups=mesh['gx'=8,'gy'=16] {'gx','gy'}, use_global_device_ids=true, to_apply=%region_0.1 | all-reduce | flops 16384 | bytes 98304 | tf_op jit(solution)/shard_map/psum | solution.py:97
  90.2 0.7 convert_bitcast_fusion
  91.0 1.2 fusion.6
  92.4 0.8 stack.128
  93.3 1.7 %collective-permute-start.2 = (bf16[8,2,64,16]{2,3,1,0:T(8,128)(2,1)S(1)}, bf16[8,2,64,16]{2,3,1,0:T(8,128)(2,1)S(1)}, u32[]{:S(2)}, u32[]{:S(2)}) collective-permute-start(bf16[8,2,64,16]{2,3,1,0:T(8,128)(2,1)S(1)} %get-tuple-element.33), channel_id=1, source_target_pairs={{0,1},{1,2},{2,3},{3,4},{4,5},{5,6},{6,7},{7,8},{8,9},{9,10},{10,1... | collective-permute-start | bytes 98312 | tf_op jit(solution)/shard_map/ppermute | solution.py:25
  96.0 0.7 fusion.28
  96.6 0.7 collective-permute-start.7
  97.4 1.0 collective-permute-start.6
  98.4 0.8 stack.125
  99.1 0.8 stack.131
  102.6 0.2 stack.115
  105.4 1.6 %stack.97 = bf16[16,4,4,1024]{3,0,2,1:T(8,128)(2,1)S(1)} concatenate(bf16[1,4,4,1024]{3,0,2,1:T(2,128)(2,1)S(1)} %stack.108, bf16[1,4,4,1024]{3,0,2,1:T(2,128)(2,1)S(1)} %stack.109, bf16[1,4,4,1024]{3,0,2,1:T(2,128)(2,1)S(1)} %stack.110, bf16[1,4,4,1024]{3,0,2,1:T(2,128)(2,1)S(1)} %stack.111, bf16[1,4,4,1024]{3,0,2,1:T(2,128)(2,1)S(1)} %stack.112, ...), dimensions={0} | concatenate | bytes 1048576 | tf_op jit(solution)/shard_map/stack | solution.py:42
  107.1 0.3 convolution_convert_fusion.1
  107.3 1.7 %reshape.83 = bf16[4,4,512,16]{3,2,1,0:T(8,128)(2,1)S(1)} reshape(bf16[4,4,8,1024]{3,2,1,0:T(8,128)(2,1)S(1)} %convolution_convert_fusion.1) | data formatting | bytes 524288 | tf_op jit(solution)/shard_map/reshape | solution.py:108
  109.1 2.2 %pad_maximum_fusion.1 = (bf16[4,4,16,256]{3,2,1,0:T(8,128)(2,1)}, bf16[4,4,16,256]{3,2,1,0:T(8,128)(2,1)}, bf16[4,4,16,256]{3,2,1,0:T(8,128)(2,1)}, bf16[4,4,16,...) fusion(bf16[6,1,16,256]{3,2,1,0:T(8,128)(2,1)} %collective-permute-done.7, ...), kind=kLoop, calls=%fused_computation.33 | loop fusion | flops 393216 | bytes 1081344 | tf_op jit(solution)/shard_map/concatenate | solution.py:23
  111.3 1.9 %stack.124 = bf16[1,4,4,4096]{3,0,2,1:T(2,128)(2,1)} reshape(bf16[4,4,16,256]{3,2,1,0:T(8,128)(2,1)} %get-tuple-element.26) | data formatting | bytes 262144 | tf_op jit(solution)/shard_map/stack | solution.py:42
  113.2 1.9 %stack.126 = bf16[1,4,4,4096]{3,0,2,1:T(2,128)(2,1)} reshape(bf16[4,4,16,256]{3,2,1,0:T(8,128)(2,1)} %get-tuple-element.6) | data formatting | bytes 262144 | tf_op jit(solution)/shard_map/stack | solution.py:42
  115.1 1.9 %stack.127 = bf16[1,4,4,4096]{3,0,2,1:T(2,128)(2,1)} reshape(bf16[4,4,16,256]{3,2,1,0:T(8,128)(2,1)} %get-tuple-element.25) | data formatting | bytes 262144 | tf_op jit(solution)/shard_map/stack | solution.py:42
  117.0 1.9 %stack.129 = bf16[1,4,4,4096]{3,0,2,1:T(2,128)(2,1)} reshape(bf16[4,4,16,256]{3,2,1,0:T(8,128)(2,1)} %get-tuple-element.7) | data formatting | bytes 262144 | tf_op jit(solution)/shard_map/stack | solution.py:42
  118.9 1.9 %stack.130 = bf16[1,4,4,4096]{3,0,2,1:T(2,128)(2,1)} reshape(bf16[4,4,16,256]{3,2,1,0:T(8,128)(2,1)} %get-tuple-element.27) | data formatting | bytes 262144 | tf_op jit(solution)/shard_map/stack | solution.py:42
  120.8 1.9 %stack.132 = bf16[1,4,4,4096]{3,0,2,1:T(2,128)(2,1)} reshape(bf16[4,4,16,256]{3,2,1,0:T(8,128)(2,1)} %get-tuple-element.5) | data formatting | bytes 262144 | tf_op jit(solution)/shard_map/stack | solution.py:42
  122.7 11.0 %stack.107 = bf16[9,4,4,4096]{3,0,2,1:T(8,128)(2,1)} concatenate(bf16[1,4,4,4096]{3,0,2,1:T(2,128)(2,1)} %stack.124, bf16[1,4,4,4096]{3,0,2,1:T(2,128)(2,1)} %stack.125, bf16[1,4,4,4096]{3,0,2,1:T(2,128)(2,1)} %stack.126, bf16[1,4,4,4096]{3,0,2,1:T(2,128)(2,1)} %stack.127, bf16[1,4,4,4096]{3,0,2,1:T(2,128)(2,1)S(1)} %copy-done.2, bf16[1,4,4,4096]{3,0,2,1:T(2,128)(2,1)} %stack.129, ...), dimensions={0} | concatenate | bytes 2359296 | tf_op jit(solution)/shard_map/stack | solution.py:42
  133.7 3.1 %convolution_convert_fusion = bf16[4,4,8,4096]{3,2,1,0:T(8,128)(2,1)} fusion(bf16[9,4,4,4096]{3,0,2,1:T(8,128)(2,1)} %stack.107, s32[4,4,8]{2,1,0:T(4,128)S(1)} %copy-done.7), kind=kOutput, calls=%fused_computation | convolution fusion | flops 9962624 | bytes 2228736 | tf_op jit(solution)/shard_map/xysr,rxyz->xysz/dot_general | solution.py:49
  136.7 10.5 %convolution_bitcast_fusion = f32[4,4,16,256]{3,2,1,0:T(8,128)S(1)} fusion(bf16[4,4,8,256,256]{4,3,2,1,0:T(8,128)(2,1)} %param.13, bf16[4,4,8,16,256]{4,2,3,1,0:T(8,128)(2,1)} %bitcast.106), kind=kOutput, calls=%fused_computation.3 | convolution fusion | flops 268435456 | bytes 18087936 | tf_op jit(solution)/shard_map/abmpq,abmvq->abvp/dot_general | solution.py:119
  147.3 2.5 %fusion = bf16[4,4,16,256]{3,2,1,0:T(8,128)(2,1)} fusion(f32[4,4,16,256]{3,2,1,0:T(8,128)S(1)} %convolution_bitcast_fusion, bf16[4,4,64,256]{3,2,1,0:T(8,128)(2,1)} %param.12, f32[4,4,64,16]{2,3,1,0:T(8,128)S(1)} %convolution_bitcast_fusion.1, bf16[4,4,512,16]{3,2,1,0:T(8,128)(2,1)S(1)} %reshape.83, bf16[4,4,64,512]{3,2,1,0:T(8,128)(2,1)S(1)} %copy-done), kind=kOutput, calls=%fused_computation.4 | convolution fusion | flops 25329664 | bytes 2293760 | tf_op jit(solution)/shard_map/abkp,abkv->abvp/dot_general | solution.py:113
  (72 shorter events, 6.7 us)
Async XLA Ops:
  0.0 147.3 %copy-start = (bf16[4,4,64,512]{3,2,1,0:T(8,128)(2,1)S(1)}, bf16[4,4,64,512]{3,2,1,0:T(8,128)(2,1)}, u32[]{:S(2)}) copy-start(bf16[4,4,64,512]{3,2,1,0:T(8,128)(2,1)} %param.16) | copy-start | bytes 3145732
  0.0 92.4 %copy-start.1 = (bf16[4,4,16,256]{3,2,1,0:T(8,128)(2,1)S(1)}, bf16[4,4,16,256]{3,2,1,0:T(8,128)(2,1)}, u32[]{:S(2)}) copy-start(bf16[4,4,16,256]{3,2,1,0:T(8,128)(2,1)} %param.11) | copy-start | bytes 393220
  0.0 92.3 %copy-start.3 = (bf16[4,4,64,64]{3,2,1,0:T(8,128)(2,1)S(1)}, bf16[4,4,64,64]{3,2,1,0:T(8,128)(2,1)}, u32[]{:S(2)}) copy-start(bf16[4,4,64,64]{3,2,1,0:T(8,128)(2,1)} %param.17) | copy-start | bytes 393220
  0.0 91.0 %copy-start.5 = (bf16[1,1,64,64]{3,2,1,0:T(8,128)(2,1)S(1)}, bf16[1,1,64,64]{3,2,1,0:T(8,128)(2,1)}, u32[]{:S(2)}) copy-start(bf16[1,1,64,64]{3,2,1,0:T(8,128)(2,1)} %param.18) | copy-start | bytes 24580
  0.9 95.0 %collective-permute-start.5 = (bf16[1,4,16,256]{3,2,1,0:T(8,128)(2,1)S(1)}, bf16[1,4,16,256]{3,2,1,0:T(8,128)(2,1)S(1)}, u32[]{:S(2)}, u32[]{:S(2)}) collective-permute-start(bf16[1,4,16,256]{3,2,1,0:T(8,128)(2,1)S(1)} %get-tuple-element.37), channel_id=1, source_target_pairs={{16,0},{32,16},{48,32},{64,48},{80,64},{96,80},{112,96},{0,112},{1... | collective-permute-start | bytes 98312 | tf_op jit(solution)/shard_map/ppermute | solution.py:27
  6.9 88.9 %collective-permute-start.4 = (bf16[1,4,16,256]{3,2,1,0:T(8,128)(2,1)S(1)}, bf16[1,4,16,256]{3,2,1,0:T(8,128)(2,1)S(1)}, u32[]{:S(2)}, u32[]{:S(2)}) collective-permute-start(bf16[1,4,16,256]{3,2,1,0:T(8,128)(2,1)S(1)} %get-tuple-element.38), channel_id=1, source_target_pairs={{0,16},{16,32},{32,48},{48,64},{64,80},{80,96},{96,112},{112,0},{1... | collective-permute-start | bytes 98312 | tf_op jit(solution)/shard_map/ppermute | solution.py:25
  8.3 84.9 %collective-permute-start.1 = (bf16[2,4,64,16]{2,3,1,0:T(8,128)(2,1)S(1)}, bf16[2,4,64,16]{2,3,1,0:T(8,128)(2,1)S(1)}, u32[]{:S(2)}, u32[]{:S(2)}) collective-permute-start(bf16[2,4,64,16]{2,3,1,0:T(8,128)(2,1)S(1)} %get-tuple-element.42), channel_id=1, source_target_pairs={{16,0},{32,16},{48,32},{64,48},{80,64},{96,80},{112,96},{0,112},{1... | collective-permute-start | bytes 49160 | tf_op jit(solution)/shard_map/ppermute | solution.py:27
  13.4 79.8 %collective-permute-start = (bf16[2,4,64,16]{2,3,1,0:T(8,128)(2,1)S(1)}, bf16[2,4,64,16]{2,3,1,0:T(8,128)(2,1)S(1)}, u32[]{:S(2)}, u32[]{:S(2)}) collective-permute-start(bf16[2,4,64,16]{2,3,1,0:T(8,128)(2,1)S(1)} %get-tuple-element.41), channel_id=1, source_target_pairs={{0,16},{16,32},{32,48},{48,64},{64,80},{80,96},{96,112},{112,0},{1... | collective-permute-start | bytes 49160 | tf_op jit(solution)/shard_map/ppermute | solution.py:25
  93.3 6.6 %collective-permute-start.3 = (bf16[8,2,64,16]{2,3,1,0:T(8,128)(2,1)S(1)}, bf16[8,2,64,16]{2,3,1,0:T(8,128)(2,1)S(1)}, u32[]{:S(2)}, u32[]{:S(2)}) collective-permute-start(bf16[8,2,64,16]{2,3,1,0:T(8,128)(2,1)S(1)} %get-tuple-element.32), channel_id=1, source_target_pairs={{1,0},{2,1},{3,2},{4,3},{5,4},{6,5},{7,6},{8,7},{9,8},{10,9},{11,1... | collective-permute-start | bytes 98312 | tf_op jit(solution)/shard_map/ppermute | solution.py:27
  93.3 6.6 %collective-permute-start.2 = (bf16[8,2,64,16]{2,3,1,0:T(8,128)(2,1)S(1)}, bf16[8,2,64,16]{2,3,1,0:T(8,128)(2,1)S(1)}, u32[]{:S(2)}, u32[]{:S(2)}) collective-permute-start(bf16[8,2,64,16]{2,3,1,0:T(8,128)(2,1)S(1)} %get-tuple-element.33), channel_id=1, source_target_pairs={{0,1},{1,2},{2,3},{3,4},{4,5},{5,6},{6,7},{7,8},{8,9},{9,10},{10,1... | collective-permute-start | bytes 98312 | tf_op jit(solution)/shard_map/ppermute | solution.py:25
  95.9 4.2 %copy-start.4 = (bf16[6,4,16,256]{3,2,1,0:T(8,128)(2,1)}, bf16[6,4,16,256]{3,2,1,0:T(8,128)(2,1)S(1)}, u32[]{:S(2)}) copy-start(bf16[6,4,16,256]{3,2,1,0:T(8,128)(2,1)S(1)} %constant_dynamic-update-slice_fusion) | copy-start | bytes 589828
  96.6 12.4 %collective-permute-start.7 = (bf16[6,1,16,256]{3,2,1,0:T(8,128)(2,1)}, bf16[6,1,16,256]{3,2,1,0:T(8,128)(2,1)}, u32[]{:S(2)}, u32[]{:S(2)}) collective-permute-start(bf16[6,1,16,256]{3,2,1,0:T(8,128)(2,1)} %get-tuple-element.28), channel_id=1, source_target_pairs={{1,0},{2,1},{3,2},{4,3},{5,4},{6,5},{7,6},{8,7},{9,8},{10,9},{11,1... | collective-permute-start | bytes 147464 | tf_op jit(solution)/shard_map/ppermute | solution.py:27
  97.4 11.7 %collective-permute-start.6 = (bf16[6,1,16,256]{3,2,1,0:T(8,128)(2,1)}, bf16[6,1,16,256]{3,2,1,0:T(8,128)(2,1)}, u32[]{:S(2)}, u32[]{:S(2)}) collective-permute-start(bf16[6,1,16,256]{3,2,1,0:T(8,128)(2,1)} %get-tuple-element.29), channel_id=1, source_target_pairs={{0,1},{1,2},{2,3},{3,4},{4,5},{5,6},{6,7},{7,8},{8,9},{9,10},{10,1... | collective-permute-start | bytes 147464 | tf_op jit(solution)/shard_map/ppermute | solution.py:25
  103.9 3.1 %copy-start.6 = (s32[4,4,8]{2,1,0:T(4,128)S(1)}, s32[4,4,8]{2,1,0:T(4,128)}, u32[]{:S(2)}) copy-start(s32[4,4,8]{2,1,0:T(4,128)} %param.15) | copy-start | bytes 1540
  109.0 13.6 %copy-start.2 = (bf16[1,4,4,4096]{3,0,2,1:T(2,128)(2,1)S(1)}, bf16[1,4,4,4096]{3,0,2,1:T(2,128)(2,1)}, u32[]{:S(2)}) copy-start(bf16[1,4,4,4096]{3,0,2,1:T(2,128)(2,1)} %stack.128) | copy-start | bytes 393220
  122.7 11.0 %copy-start.7 = (s32[4,4,8]{2,1,0:T(4,128)S(1)}, s32[4,4,8]{2,1,0:T(4,128)}, u32[]{:S(2)}) copy-start(s32[4,4,8]{2,1,0:T(4,128)} %param.14) | copy-start | bytes 1540
where the time goes:
time: 153 us; the launch traced here: 150 us
  blocking collectives  71.5 us (47%)
  local copies, waits for them, and re-layouts  37.1 us (24%)
  matrix products  20.3 us (13%)
  starting transfers between devices  14.7 us (10%)
  other arithmetic  3.88 us (3%)
  between operations  2.34 us (2%)
    psum x1, blocking collectives, local(): coarse_sum = lax.psum(placed, ('gx', 'gy'))  71.5 us
    another operation x27, local copies, waits for them, and re-layouts, shifted_stack(): stacked = jnp.stack(pieces)  29.2 us
    ppermute x4, starting transfers between devices, with_halo(): lax.ppermute(head, axis, [((i + 1) % count, i) for i in range(count)])  12 us
    dot_general x1, matrix products, local(): jnp.einsum('abmpq,abmvq->abvp', near_blocks, near_charges, preferred_elem...  10.5 us
    dot_general x2, matrix products, pick_rows(): jnp.einsum('xysr,rxyz->xysz', one_hot, stacked, preferred_element_type=jn...  3.34 us
  transfers between devices with their start and end apart: 8, of which 0 were waited for; matrix products, arithmetic and copies ran while one was open for 13% of the time, Pallas kernels for 0%

commit v1 on v0

v1 whole, which is shorter than its diff:
```python
import functools

import jax
import jax.numpy as jnp
from jax import lax
from jax.experimental import pallas as pl
from jax.experimental.pallas import tpu as pltpu
from jax.sharding import PartitionSpec as P

MESH = pl.DeviceIdType.MESH
NT = (((1,), (1,)), ((), ()))
NN = (((1,), (0,)), ((), ()))
bf16 = jnp.bfloat16
f32 = jnp.float32

SIDES = [(sx, sy) for sx in (-1, 0, 1) for sy in (-1, 0, 1) if (sx, sy) != (0, 0)]


def dot(left, right, dims):
    return lax.dot_general(left, right, dims, preferred_element_type=f32)


def strip(side, depth, count):
    if side == 0:
        return pl.ds(0, count), pl.ds(depth, count)
    if side > 0:
        return pl.ds(count - depth, depth), pl.ds(0, depth)
    return pl.ds(0, depth), pl.ds(count + depth, depth)


def kernel(
    n_gx,
    n_gy,
    charges,
    basis,
    near_blocks,
    near_list,
    far_list,
    coupling,
    transfer,
    coarse_transfer,
    coarse_group,
    coarse_pattern,
    coarse_coupling,
    out,
    charge_pad,
    basis_v,
    near_v,
    near_s,
    far_s,
    coupling_v,
    transfer_v,
    ct_v,
    group_s,
    pattern_s,
    weight_v,
    coef_pad,
    coupled_v,
    total_v,
    out_v,
    term_v,
    part_v,
    far_v,
    load_sem,
    near_sem,
    out_sem,
    charge_send,
    charge_recv,
    coef_send,
    coef_recv,
    stage_send,
    stage_recv,
):
    lx, ly = charges.shape[0], charges.shape[1]
    leaves = [(x, y) for x in range(lx) for y in range(ly)]
    rank = basis.shape[2]
    gx = lax.axis_index("gx")
    gy = lax.axis_index("gy")

    def beside(sx, sy):
        return lax.rem(gx + sx + n_gx, n_gx), lax.rem(gy + sy + n_gy, n_gy)

    row_peers = [beside(0, step) for step in range(1, n_gy)]
    column_peers = [beside(step, 0) for step in range(1, n_gx)]
    corners = [beside(sx, sy) for sx, sy in SIDES if sx != 0 and sy != 0]

    barrier = pltpu.get_barrier_semaphore()
    for peer in row_peers + column_peers + corners:
        pl.semaphore_signal(barrier, inc=1, device_id=peer, device_id_type=MESH)

    loads = [
        pltpu.make_async_copy(source, target, load_sem.at[number])
        for number, (source, target) in enumerate(
            [
                (charges, charge_pad.at[pl.ds(1, lx), pl.ds(1, ly)]),
                (basis, basis_v),
                (transfer, transfer_v),
                (coarse_transfer.at[0, 0], ct_v),
                (coarse_group, group_s),
                (coarse_pattern, pattern_s),
                (near_list, near_s),
                (far_list, far_s),
                (coarse_coupling.at[gy], weight_v),
                (coupling, coupling_v),
            ]
        )
    ]
    for load in loads:
        load.start()
    for number, (x, y) in enumerate(leaves):
        pltpu.make_async_copy(near_blocks.at[x, y], near_v.at[number], near_sem.at[number]).start()

    pl.semaphore_wait(barrier, len(row_peers) + len(column_peers) + len(corners))

    charge_copies = []
    for number, (sx, sy) in enumerate(SIDES):
        from_x, to_x = strip(sx, 1, lx)
        from_y, to_y = strip(sy, 1, ly)
        charge_copies.append(
            pltpu.make_async_remote_copy(
                src_ref=charges.at[from_x, from_y],
                dst_ref=charge_pad.at[to_x, to_y],
                send_sem=charge_send.at[number],
                recv_sem=charge_recv.at[number],
                device_id=beside(sx, sy),
                device_id_type=MESH,
            )
        )
    for copy in charge_copies:
        copy.start()

    for load in loads[:4]:
        load.wait()
    cluster = jnp.zeros((out.shape[2], rank), f32)
    for x, y in leaves:
        doubled = jnp.concatenate([basis_v[x, y], basis_v[x, y]], axis=0)
        coef = dot(charge_pad[1 + x, 1 + y], doubled, NT).astype(bf16)
        coef_pad[2 + x, 2 + y] = coef
        cluster += dot(coef[:, :rank], transfer_v[x, y], NT)
    own = ct_v[...]
    term = dot(cluster.astype(bf16), jnp.concatenate([own, own], axis=0), NT).astype(bf16)
    term_v[gy] = term

    def exchange(buffer, slot, peers, stage):
        copies = [
            pltpu.make_async_remote_copy(
                src_ref=buffer.at[slot],
                dst_ref=buffer.at[slot],
                send_sem=stage_send.at[stage],
                recv_sem=stage_recv.at[stage],
                device_id=peer,
                device_id_type=MESH,
            )
            for peer in peers
        ]
        for copy in copies:
            copy.start()

    def all_of(buffer, count, sem):
        view = buffer.at[pl.ds(0, count)]
        pltpu.make_async_copy(view, view, sem).wait()

    exchange(term_v, gy, row_peers, 0)

    coef_copies = []
    for number, (sx, sy) in enumerate(SIDES):
        from_x, to_x = strip(sx, 2, lx)
        from_y, to_y = strip(sy, 2, ly)
        coef_copies.append(
            pltpu.make_async_remote_copy(
                src_ref=coef_pad.at[pl.ds(2 + from_x.start, from_x.size), pl.ds(2 + from_y.start, from_y.size)],
                dst_ref=coef_pad.at[to_x, to_y],
                send_sem=coef_send.at[number],
                recv_sem=coef_recv.at[number],
                device_id=beside(sx, sy),
                device_id_type=MESH,
            )
        )
    for copy in coef_copies:
        copy.start()

    for load in loads[4:]:
        load.wait()
    for copy in charge_copies:
        copy.wait_recv()

    together = 2

    def near_pass(first, last):
        def body(step, carry):
            numbers = [step * together + h for h in range(together)]
            for number in numbers:
                pltpu.make_async_copy(near_v.at[number], near_v.at[number], near_sem.at[number]).wait()
            for number in numbers:
                x, y = number // ly, lax.rem(number, ly)
                total = jnp.zeros((out.shape[2], out.shape[3]), f32)
                for entry in range(near_v.shape[1]):
                    place = near_s[x, y, entry]
                    down = lax.shift_right_logical(place * 11, 5)
                    total += dot(charge_pad[x + down, y + place - 3 * down], near_v[number, entry], NT)
                total_v[number] = total
            return carry

        lax.fori_loop(first // together, last // together, body, 0)

    near_pass(0, 4)

    all_of(term_v, n_gy - 1, stage_recv.at[0])
    lane_half = (lax.broadcasted_iota(jnp.int32, (1, 2 * rank), 1) >= rank).astype(jnp.int32)
    terms = [term_v[slot].astype(f32) for slot in range(n_gy)]
    groups = [group_s[gx * n_gy + slot] for slot in range(n_gy)]
    sums = []
    for pair in range(n_gy // 2):
        total = jnp.zeros((out.shape[2], 2 * rank), f32)
        for slot in range(n_gy):
            total += jnp.where(lane_half == groups[slot] - 2 * pair, terms[slot], 0.0)
        low, high = pattern_s[gy, 2 * pair], pattern_s[gy, 2 * pair + 1]
        allowed = jnp.where(lane_half == 0, low, high) != 0
        sums.append(jnp.where(allowed, total, 0.0).astype(bf16))
    weight = weight_v[...]
    part_v[gx] = dot(jnp.concatenate(sums, axis=1), jnp.concatenate([weight, weight], axis=0), NT)
    exchange(part_v, gx, column_peers, 1)

    near_pass(4, 8)

    for copy in coef_copies:
        copy.wait_recv()
    left_half = lax.broadcasted_iota(jnp.int32, (out.shape[2], 2 * rank), 1) < rank

    def couple(step, carry):
        for h in range(ly):
            x, y = step, h
            picked = []
            for entry in range(far_s.shape[2]):
                place = far_s[x, y, entry]
                offset = jnp.minimum(jnp.maximum(place - 18, 4 * place - 30), place + 3) + 18
                down = lax.shift_right_logical(offset, 3)
                picked.append(coef_pad[x + down, y + offset - 8 * down])
            chosen = [
                jnp.where(left_half, picked[2 * pair].astype(f32), picked[2 * pair + 1].astype(f32)).astype(bf16)
                for pair in range(len(picked) // 2)
            ]
            coupled_v[x, y] = dot(jnp.concatenate(chosen, axis=1), coupling_v[x, y], NT)
        return carry

    lax.fori_loop(0, lx, couple, 0)

    all_of(part_v, n_gx - 1, stage_recv.at[1])
    far_sum = part_v[0]
    for slot in range(1, n_gx):
        far_sum += part_v[slot]
    far_v[gy] = far_sum.astype(bf16)
    exchange(far_v, gy, row_peers, 2)

    near_pass(8, 16)

    all_of(far_v, n_gy - 1, stage_recv.at[2])
    my_group = group_s[gx * n_gy + gy]
    cluster_far = dot(far_v[my_group][:, :rank], own, NN).astype(bf16)

    def finish(step, carry):
        for h in range(ly):
            x, y = step, h
            leaf_far = (coupled_v[x, y] + dot(cluster_far, transfer_v[x, y], NN)).astype(bf16)
            out_v[x, y] = (total_v[x * ly + y] + dot(leaf_far, basis_v[x, y], NN)).astype(bf16)
        return carry

    lax.fori_loop(0, lx, finish, 0)

    store = pltpu.make_async_copy(out_v, out, out_sem)
    store.start()
    all_of(term_v, n_gy - 1, stage_send.at[0])
    all_of(part_v, n_gx - 1, stage_send.at[1])
    all_of(far_v, n_gy - 1, stage_send.at[2])
    for copy in charge_copies + coef_copies:
        copy.wait_send()
    store.wait()


def local(n_gx, n_gy, *arrays):
    charges, basis, near_blocks, near_list, far_list, coupling, transfer, coarse_transfer = arrays[:8]
    coarse_group, coarse_pattern, coarse_coupling = arrays[8:]
    lx, ly, vectors, points = charges.shape
    rank = basis.shape[2]
    halves = 2 * rank
    scratch = [
        pltpu.VMEM((lx + 2, ly + 2, vectors, points), bf16),
        pltpu.VMEM(basis.shape, bf16),
        pltpu.VMEM((lx * ly,) + near_blocks.shape[2:], bf16),
        pltpu.SMEM(near_list.shape, jnp.int32),
        pltpu.SMEM(far_list.shape, jnp.int32),
        pltpu.VMEM(coupling.shape, bf16),
        pltpu.VMEM(transfer.shape, bf16),
        pltpu.VMEM(coarse_transfer.shape[2:], bf16),
        pltpu.SMEM(coarse_group.shape, jnp.int32),
        pltpu.SMEM(coarse_pattern.shape, jnp.int32),
        pltpu.VMEM(coarse_coupling.shape[1:], bf16),
        pltpu.VMEM((lx + 4, ly + 4, vectors, halves), bf16),
        pltpu.VMEM((lx, ly, vectors, rank), f32),
        pltpu.VMEM((lx * ly, vectors, points), f32),
        pltpu.VMEM((lx, ly, vectors, points), bf16),
        pltpu.VMEM((n_gy, vectors, halves), bf16),
        pltpu.VMEM((n_gx, vectors, halves), f32),
        pltpu.VMEM((n_gy, vectors, halves), bf16),
        pltpu.SemaphoreType.DMA((10,)),
        pltpu.SemaphoreType.DMA((lx * ly,)),
        pltpu.SemaphoreType.DMA,
        pltpu.SemaphoreType.DMA((len(SIDES),)),
        pltpu.SemaphoreType.DMA((len(SIDES),)),
        pltpu.SemaphoreType.DMA((len(SIDES),)),
        pltpu.SemaphoreType.DMA((len(SIDES),)),
        pltpu.SemaphoreType.DMA((3,)),
        pltpu.SemaphoreType.DMA((3,)),
    ]
    return pl.pallas_call(
        functools.partial(kernel, n_gx, n_gy),
        out_shape=jax.ShapeDtypeStruct(charges.shape, bf16),
        in_specs=[pl.BlockSpec(memory_space=pltpu.HBM)] * len(arrays),
        out_specs=pl.BlockSpec(memory_space=pl.ANY),
        scratch_shapes=scratch,
        compiler_params=pltpu.CompilerParams(
            collective_id=0, has_side_effects=True, vmem_limit_bytes=60 * 2**20
        ),
    )(*arrays)


def solution(mesh):
    split = P("gx", "gy")
    return jax.shard_map(
        functools.partial(local, mesh.shape["gx"], mesh.shape["gy"]),
        mesh=mesh,
        in_specs=(split,) * 8 + (P(), P(), P()),
        out_specs=split,
        check_vma=False,
    )
```

time: 153 us -> 28.1 us (0.18); the launches traced: 150 us -> 28 us
  blocking collectives: 71.5 us -> 0 us
  local copies, waits for them, and re-layouts: 37.1 us -> 1.57 us
  Pallas kernels: 0 us -> 26.4 us
  matrix products: 20.3 us -> 0 us
  starting transfers between devices: 14.7 us -> 0 us
  other arithmetic: 3.88 us -> 0 us
  between operations: 2.34 us -> 0.01 us
    psum x1 -> x0, blocking collectives: 71.5 us -> none  [local(): coarse_sum = lax.psum(placed, ('gx', 'gy'))]
    another operation x27 -> x0, local copies, waits for them, and re-layouts: 29.2 us -> none  [shifted_stack(): stacked = jnp.stack(pieces)]
    pallas_call x0 -> x1, Pallas kernels: none -> 26.4 us  [local(): pl.pallas_call(functools.partial(kernel, n_gx, n_gy), out_shape=jax.Shape...]
    dot_general x8 -> x0, matrix products: 20.3 us -> none  [the longest x1 10.5 us: local(): jnp.einsum('abmpq,abmvq->abvp', near_blocks, near_charges, preferred_elem...]
    ppermute x8 -> x0, starting transfers between devices: 14.7 us -> none  [the longest x4 12 us: with_halo(): lax.ppermute(head, axis, [((i + 1) % count, i) for i in range(count)])]
    slice x21 -> x0, local copies, waits for them, and re-layouts: 4.6 us -> none  [the longest x17 2.99 us: shifted_stack(): padded[margin + shift_x:margin + shift_x + leaves_x, margin + shift_y:mar...]
    concatenate x5 -> x0, other arithmetic: 2.4 us -> none  [with_halo(): jnp.concatenate([lax.ppermute(tail, axis, [(i, (i + 1) % count) for i in...]
    reshape x1 -> x0, local copies, waits for them, and re-layouts: 1.7 us -> none  [local(): pick_rows(cycle_coef, far_list)]
  transfers between devices with their start and end apart: 8 -> 0, of which waited for: 0 -> 0; matrix products, arithmetic and copies ran while one was open for 13% -> 0% of each run, Pallas kernels for 0% -> 0%
where the time goes in v1:
time: 28.1 us; the launch traced here: 28 us
  Pallas kernels  26.4 us (94%)
  local copies, waits for them, and re-layouts  1.57 us (6%)
    pallas_call x1, Pallas kernels, local(): pl.pallas_call(functools.partial(kernel, n_gx, n_gy), out_shape=jax.Shape...  26.4 us
    unnamed x1, local copies, waits for them, and re-layouts  1.57 us

profile of v1, /device:TPU:1, one launch (start us, length us, event | category | flops | bytes accessed | tf_op | source)
XLA Modules:
  0.0 28.0 jit_solution(16273658445114485832)
XLA Ops:
  0.0 26.4 %shard_map.109 = bf16[4,4,16,256]{3,2,1,0:T(8,128)(2,1)} custom-call(bf16[4,4,16,256]{3,2,1,0:T(8,128)(2,1)} %charges.1, bf16[4,4,64,256]{3,2,1,0:T(8,128)(2,1)} %basis.1, bf16[4,4,8,256,256]{4,3,2,1,0:T(8,128)(2,1)} %near_blocks.1, s32[4,4,8]{2,1,0:T(4,128)} %near_list.1, s32[4,4,8]{2,1,0:T(4,128)} %far_list.1, bf16[4,4,64,512]{3,2,1,0:T(8,128)(2,1)} %coupling.1, ...), custom_call_target="tpu_custom_call" | custom-call | tf_op jit(solution)/shard_map/pallas_call | solution.py:315
  26.4 1.6 %copy.13 = bf16[4,4,16,256]{3,2,1,0:T(8,128)(2,1)} copy(bf16[4,4,16,256]{3,2,1,0:T(8,128)(2,1)} %shard_map.109) | data formatting | bytes 262144

commit v2 on v1

v2 whole, which is shorter than its diff:
```python
import functools

import jax
import jax.numpy as jnp
from jax import lax
from jax.experimental import pallas as pl
from jax.experimental.pallas import tpu as pltpu
from jax.sharding import PartitionSpec as P

MESH = pl.DeviceIdType.MESH
NT = (((1,), (1,)), ((), ()))
NN = (((1,), (0,)), ((), ()))
bf16 = jnp.bfloat16
f32 = jnp.float32

SIDES = [(-1, 0), (1, 0), (0, -1), (0, 1), (-1, -1), (-1, 1), (1, -1), (1, 1)]
PAIRS = [
    ((1, 1), (1, 2)),
    ((2, 1), (2, 2)),
    ((3, 1), (3, 2)),
    ((0, 1), (0, 2)),
    ((1, 3), (2, 3)),
    ((1, 0), (2, 0)),
    ((0, 0), (0, 3)),
    ((3, 0), (3, 3)),
]
INNER = 2
COARSE_AT = 4
SPLIT = 4


def dot(left, right, dims):
    return lax.dot_general(left, right, dims, preferred_element_type=f32)


def strip(side, depth, count):
    if side == 0:
        return 0, count, depth
    if side > 0:
        return count - depth, depth, 0
    return 0, depth, count + depth


def choose(step, values):
    chosen = jnp.int32(values[0])
    for number, value in enumerate(values):
        if value != values[0]:
            chosen = jnp.where(step == number, value, chosen)
    return chosen


def kernel(
    n_gx,
    n_gy,
    charges,
    basis,
    near_blocks,
    near_list,
    far_list,
    coupling,
    transfer,
    coarse_transfer,
    coarse_group,
    coarse_pattern,
    coarse_coupling,
    out,
    charge_pad,
    land_x,
    land_y,
    land_corner,
    basis_v,
    near_v,
    near_s,
    far_s,
    coupling_v,
    transfer_v,
    ct_v,
    group_s,
    pattern_s,
    weight_v,
    coef_pad,
    fold_v,
    total_v,
    term_v,
    part_v,
    far_v,
    load_sem,
    near_sem,
    charge_send,
    charge_recv,
    coef_send,
    coef_recv,
    stage_send,
    stage_recv,
):
    lx, ly = charges.shape[0], charges.shape[1]
    vectors, points = charges.shape[2], charges.shape[3]
    leaves = [(x, y) for x in range(lx) for y in range(ly)]
    rank = basis.shape[2]
    gx = lax.axis_index("gx")
    gy = lax.axis_index("gy")

    def beside(sx, sy):
        return lax.rem(gx + sx + n_gx, n_gx), lax.rem(gy + sy + n_gy, n_gy)

    sub_x, sub_y = n_gx // SPLIT, n_gy // SPLIT
    n_plane, n_line = sub_y * SPLIT, sub_x * SPLIT

    def plane_peer(step):
        number = lax.rem(lax.rem(gx, SPLIT) * sub_y + gy // SPLIT + step + n_plane, n_plane)
        return gx // SPLIT * SPLIT + number // sub_y, lax.rem(number, sub_y) * SPLIT + lax.rem(gy, SPLIT)

    def line_peer(step):
        number = lax.rem(gx // SPLIT * SPLIT + lax.rem(gy, SPLIT) + step + n_line, n_line)
        return number // SPLIT * SPLIT + lax.rem(gx, SPLIT), gy // SPLIT * SPLIT + lax.rem(number, SPLIT)

    def group_of(device):
        return group_s[device[0] * n_gy + device[1]]

    plane = [plane_peer(step) for step in range(1, n_plane)]
    line = [line_peer(step) for step in range(1, n_line)]
    around = [beside(sx, sy) for sx, sy in SIDES]

    loads = [
        pltpu.make_async_copy(source, target, load_sem.at[number])
        for number, (source, target) in enumerate(
            [
                (charges, charge_pad.at[pl.ds(1, lx), pl.ds(1, ly)]),
                (basis, basis_v),
                (transfer, transfer_v),
                (coarse_transfer.at[0, 0], ct_v),
                (near_list, near_s),
                (coarse_group, group_s),
                (coarse_pattern, pattern_s),
                (far_list, far_s),
                (coarse_coupling, weight_v),
                (coupling, coupling_v),
            ]
        )
    ]
    order = [leaf for pair in PAIRS for leaf in pair]

    def near_start(first, last):
        for number in range(first, last):
            x, y = order[number]
            pltpu.make_async_copy(near_blocks.at[x, y], near_v.at[number], near_sem.at[number]).start()

    for load in loads[:8]:
        load.start()

    barrier = pltpu.get_barrier_semaphore()
    for peer in plane + line + around:
        pl.semaphore_signal(barrier, inc=1, device_id=peer, device_id_type=MESH)

    for load in loads[:4]:
        load.wait()
    cluster = jnp.zeros((vectors, rank), f32)
    for x, y in leaves:
        doubled = jnp.concatenate([basis_v[x, y], basis_v[x, y]], axis=0)
        coef = dot(charge_pad[1 + x, 1 + y], doubled, NT).astype(bf16)
        coef_pad[2 + x, 2 + y] = coef
        cluster += dot(coef[:, :rank], transfer_v[x, y], NT)
    own = ct_v[...]
    term_v[0] = dot(cluster.astype(bf16), jnp.concatenate([own, own], axis=0), NT).astype(bf16)

    pl.semaphore_wait(barrier, len(plane) + len(line) + len(around))

    def remote(source, target, send, recv, peer):
        return pltpu.make_async_remote_copy(
            src_ref=source, dst_ref=target, send_sem=send, recv_sem=recv, device_id=peer, device_id_type=MESH
        )

    def all_of(buffer, sem):
        view = buffer.at[pl.ds(1, buffer.shape[0] - 1)]
        pltpu.make_async_copy(view, view, sem).wait()

    for step, peer in enumerate(plane, 1):
        remote(term_v.at[0], term_v.at[step], stage_send.at[0], stage_recv.at[0], peer).start()

    charge_copies, coef_copies, landed = [], [], []
    for number, (sx, sy) in enumerate(SIDES):
        at_x, many_x, to_x = strip(sx, 1, lx)
        at_y, many_y, to_y = strip(sy, 1, ly)
        land = land_x.at[number] if number < 2 else land_y.at[number - 2] if number < 4 else land_corner.at[number - 4]
        landed.append((land, many_x, many_y, to_x, to_y))
        charge_copies.append(
            remote(
                charge_pad.at[pl.ds(1 + at_x, many_x), pl.ds(1 + at_y, many_y)],
                land,
                charge_send.at[number],
                charge_recv.at[number],
                beside(sx, sy),
            )
        )
        at_x, many_x, to_x = strip(sx, 2, lx)
        at_y, many_y, to_y = strip(sy, 2, ly)
        coef_copies.append(
            remote(
                coef_pad.at[pl.ds(2 + at_x, many_x), pl.ds(2 + at_y, many_y)],
                coef_pad.at[pl.ds(to_x, many_x), pl.ds(to_y, many_y)],
                coef_send.at[number],
                coef_recv.at[number],
                beside(sx, sy),
            )
        )
    for copy in charge_copies + coef_copies:
        copy.start()

    near_start(0, 2 * INNER)
    loads[8].start()
    near_start(2 * INNER, 8)
    loads[9].start()
    for load in loads[4:8]:
        load.wait()

    def fold(x, carry):
        for y in range(ly):
            down = dot(own, transfer_v[x, y], NN).astype(bf16)
            fold_v[x, y] = dot(down, basis_v[x, y], NN).astype(bf16)
        return carry

    lax.fori_loop(0, lx, fold, 0)

    def take(number):
        charge_copies[number].wait_recv()
        land, many_x, many_y, to_x, to_y = landed[number]
        for x in range(many_x):
            for y in range(many_y):
                charge_pad[to_x + x, to_y + y] = land[x, y]

    def coarse():
        loads[8].wait()
        all_of(term_v, stage_recv.at[0])
        half = (lax.broadcasted_iota(jnp.int32, (1, 2 * rank), 1) >= rank).astype(jnp.int32)
        terms = [term_v[step].astype(f32) for step in range(n_plane)]
        groups = [group_of(plane_peer(-step)) for step in range(n_plane)]
        sums = []
        for pair in range(weight_v.shape[0] // 2):
            total = jnp.zeros((vectors, 2 * rank), f32)
            for step in range(n_plane):
                total += jnp.where(half == groups[step] - 2 * pair, terms[step], 0.0)
            sums.append(total)
        for step in range(n_line):
            group = group_of(line_peer(step))
            allowed = []
            for pair, total in enumerate(sums):
                kept = jnp.where(half == 0, pattern_s[group, 2 * pair], pattern_s[group, 2 * pair + 1]) != 0
                allowed.append(jnp.where(kept, total, 0.0).astype(bf16))
            part = dot(jnp.concatenate(allowed, axis=1), weight_v[group], NT)
            part = jnp.concatenate([part, jnp.zeros_like(part)], axis=1)
            if step == 0:
                far_v[0] = part
            else:
                part_v[step] = part
        for step, peer in enumerate(line, 1):
            remote(part_v.at[step], far_v.at[step], stage_send.at[1], stage_recv.at[1], peer).start()

    def near_leaf(slot, x, y):
        total = jnp.zeros((vectors, points), f32)
        for entry in range(near_v.shape[1]):
            place = near_s[x, y, entry]
            down = lax.shift_right_logical(place * 11, 5)
            total += dot(charge_pad[x + down, y + place - 3 * down], near_v[slot, entry], NT)
        total_v[x, y] = total

    def near(step, carry):
        for number in range(len(SIDES) // 2):
            pl.when(step == INNER + number)(functools.partial(take, number))

        pl.when(step == COARSE_AT)(coarse)

        @pl.when(step == INNER)
        def _():
            near_start(8, len(order))

        slots = [2 * step + h for h in range(2)]
        for slot in slots:
            pltpu.make_async_copy(near_v.at[slot], near_v.at[slot], near_sem.at[slot]).wait()
        for h, slot in enumerate(slots):
            near_leaf(slot, choose(step, [pair[h][0] for pair in PAIRS]), choose(step, [pair[h][1] for pair in PAIRS]))
        return carry

    lax.fori_loop(0, len(PAIRS) - 2, near, 0)
    for number in range(len(SIDES) // 2, len(SIDES)):
        take(number)

    loads[9].wait()
    for copy in coef_copies:
        copy.wait_recv()
    left = lax.broadcasted_iota(jnp.int32, (vectors, 2 * rank), 1) < rank

    def couple(x, carry):
        for y in range(ly):
            picked = []
            for entry in range(far_s.shape[2]):
                place = far_s[x, y, entry]
                offset = jnp.minimum(jnp.maximum(place - 18, 4 * place - 30), place + 3) + 18
                down = lax.shift_right_logical(offset, 3)
                picked.append(coef_pad[x + down, y + offset - 8 * down].astype(f32))
            chosen = [
                jnp.where(left, picked[2 * pair], picked[2 * pair + 1]).astype(bf16) for pair in range(len(picked) // 2)
            ]
            coupled = dot(jnp.concatenate(chosen, axis=1), coupling_v[x, y], NT).astype(bf16)
            total_v[x, y] += dot(coupled, basis_v[x, y], NN)
        return carry

    corner_slots = range(2 * len(PAIRS) - 4, 2 * len(PAIRS))
    for slot in corner_slots:
        pltpu.make_async_copy(near_v.at[slot], near_v.at[slot], near_sem.at[slot]).wait()
    for slot in corner_slots:
        near_leaf(slot, *order[slot])
    for x in range(lx):
        couple(x, 0)

    all_of(far_v, stage_recv.at[1])
    far = far_v[0]
    for step in range(1, n_line):
        far += far_v[step]
    far = far[:, :rank].astype(bf16)
    for x, y in leaves:
        out[x, y] = (total_v[x, y] + dot(far, fold_v[x, y], NN)).astype(bf16)

    all_of(term_v, stage_send.at[0])
    all_of(part_v, stage_send.at[1])
    for copy in charge_copies + coef_copies:
        copy.wait_send()


def local(n_gx, n_gy, *arrays):
    charges, basis, near_blocks, near_list, far_list, coupling, transfer, coarse_transfer = arrays[:8]
    coarse_group, coarse_pattern, coarse_coupling = arrays[8:]
    lx, ly, vectors, points = charges.shape
    halves = 2 * basis.shape[2]
    n_plane, n_line = n_gy // SPLIT * SPLIT, n_gx // SPLIT * SPLIT
    sides = len(SIDES)
    scratch = [
        pltpu.VMEM((lx + 2, ly + 2, vectors, points), bf16),
        pltpu.VMEM((2, 1, ly, vectors, points), bf16),
        pltpu.VMEM((2, lx, 1, vectors, points), bf16),
        pltpu.VMEM((4, 1, 1, vectors, points), bf16),
        pltpu.VMEM(basis.shape, bf16),
        pltpu.VMEM((lx * ly,) + near_blocks.shape[2:], bf16),
        pltpu.SMEM(near_list.shape, jnp.int32),
        pltpu.SMEM(far_list.shape, jnp.int32),
        pltpu.VMEM(coupling.shape, bf16),
        pltpu.VMEM(transfer.shape, bf16),
        pltpu.VMEM(coarse_transfer.shape[2:], bf16),
        pltpu.SMEM(coarse_group.shape, jnp.int32),
        pltpu.SMEM(coarse_pattern.shape, jnp.int32),
        pltpu.VMEM(coarse_coupling.shape, bf16),
        pltpu.VMEM((lx + 4, ly + 4, vectors, halves), bf16),
        pltpu.VMEM(basis.shape, bf16),
        pltpu.VMEM((lx, ly, vectors, points), f32),
        pltpu.VMEM((n_plane, vectors, halves), bf16),
        pltpu.VMEM((n_line, vectors, halves), f32),
        pltpu.VMEM((n_line, vectors, halves), f32),
        pltpu.SemaphoreType.DMA((10,)),
        pltpu.SemaphoreType.DMA((lx * ly,)),
        pltpu.SemaphoreType.DMA((sides,)),
        pltpu.SemaphoreType.DMA((sides,)),
        pltpu.SemaphoreType.DMA((sides,)),
        pltpu.SemaphoreType.DMA((sides,)),
        pltpu.SemaphoreType.DMA((2,)),
        pltpu.SemaphoreType.DMA((2,)),
    ]
    return pl.pallas_call(
        functools.partial(kernel, n_gx, n_gy),
        out_shape=pltpu.VMEM(charges.shape, bf16),
        in_specs=[pl.BlockSpec(memory_space=pl.ANY)] * len(arrays),
        out_specs=pl.BlockSpec(memory_space=pltpu.VMEM),
        scratch_shapes=scratch,
        compiler_params=pltpu.CompilerParams(
            collective_id=0, has_side_effects=True, vmem_limit_bytes=56 * 2**20
        ),
    )(*arrays)


def solution(mesh):
    split = P("gx", "gy")
    return jax.shard_map(
        functools.partial(local, mesh.shape["gx"], mesh.shape["gy"]),
        mesh=mesh,
        in_specs=(split,) * 8 + (P(), P(), P()),
        out_specs=split,
        check_vma=False,
    )
```

time: 28.1 us -> 20.1 us (0.72)
  Pallas kernels: 26.4 us -> 19.1 us
  local copies, waits for them, and re-layouts: 1.57 us -> 0.66 us
    pallas_call x1, Pallas kernels: 26.4 us -> 19.1 us  [local(): pl.pallas_call(functools.partial(kernel, n_gx, n_gy), out_shape=pltpu.VME...]
    unnamed x1, local copies, waits for them, and re-layouts: 1.57 us -> 0.66 us
where the time goes in v2:
time: 20.1 us; the launch traced here: 19.8 us
  Pallas kernels  19.1 us (95%)
  local copies, waits for them, and re-layouts  0.66 us (3%)
    pallas_call x1, Pallas kernels, local(): pl.pallas_call(functools.partial(kernel, n_gx, n_gy), out_shape=pltpu.VME...  19.1 us
    unnamed x1, local copies, waits for them, and re-layouts  0.66 us

profile of v2, /device:TPU:1, one launch (start us, length us, event | category | flops | bytes accessed | tf_op | source)
XLA Modules:
  0.0 19.8 jit_solution(11134770593804050435)
XLA Ops:
  0.0 19.1 %shard_map.109 = bf16[4,4,16,256]{3,2,1,0:T(8,128)(2,1)S(1)} custom-call(bf16[4,4,16,256]{3,2,1,0:T(8,128)(2,1)} %charges.1, bf16[4,4,64,256]{3,2,1,0:T(8,128)(2,1)} %basis.1, bf16[4,4,8,256,256]{4,3,2,1,0:T(8,128)(2,1)} %near_blocks.1, s32[4,4,8]{2,1,0:T(4,128)} %near_list.1, s32[4,4,8]{2,1,0:T(4,128)} %far_list.1, bf16[4,4,64,512]{3,2,1,0:T(8,128)(2,1)} %coupling.1, ...), custom_call_target="tpu_custom_call" | custom-call | tf_op jit(solution)/shard_map/pallas_call | solution.py:366
  19.1 0.7 %copy.13 = bf16[4,4,16,256]{3,2,1,0:T(8,128)(2,1)} copy(bf16[4,4,16,256]{3,2,1,0:T(8,128)(2,1)S(1)} %shard_map.109) | data formatting | bytes 262144

commit v3 on v2

--- a/solution.py
+++ b/solution.py
@@ -25,7 +25,7 @@
     ((3, 0), (3, 3)),
 ]
 INNER = 2
-COARSE_AT = 4
+COARSE_AT = 3
 SPLIT = 4
 
 
@@ -64,6 +64,7 @@
     coarse_pattern,
     coarse_coupling,
     out,
+    charge_v,
     charge_pad,
     land_x,
     land_y,
@@ -72,13 +73,20 @@
     near_v,
     near_s,
     far_s,
+    near_at,
+    far_at,
     coupling_v,
     transfer_v,
     ct_v,
     group_s,
     pattern_s,
     weight_v,
+    allowed_v,
+    coef_v,
     coef_pad,
+    coef_x,
+    coef_y,
+    coef_corner,
     fold_v,
     total_v,
     term_v,
@@ -117,15 +125,20 @@
     def group_of(device):
         return group_s[device[0] * n_gy + device[1]]
 
-    plane = [plane_peer(step) for step in range(1, n_plane)]
-    line = [line_peer(step) for step in range(1, n_line)]
+    def ring(step, size):
+        return min(step, size - step)
+
+    plane_steps = sorted(range(1, n_plane), key=lambda step: -ring(step // sub_y, SPLIT) - ring(step % sub_y, sub_y))
+    line_steps = sorted(range(1, n_line), key=lambda step: -ring(step, n_line))
+    plane = [plane_peer(step) for step in plane_steps]
+    line = [line_peer(step) for step in line_steps]
     around = [beside(sx, sy) for sx, sy in SIDES]
 
     loads = [
         pltpu.make_async_copy(source, target, load_sem.at[number])
         for number, (source, target) in enumerate(
             [
-                (charges, charge_pad.at[pl.ds(1, lx), pl.ds(1, ly)]),
+                (charges, charge_v),
                 (basis, basis_v),
                 (transfer, transfer_v),
                 (coarse_transfer.at[0, 0], ct_v),
@@ -157,12 +170,16 @@
     cluster = jnp.zeros((vectors, rank), f32)
     for x, y in leaves:
         doubled = jnp.concatenate([basis_v[x, y], basis_v[x, y]], axis=0)
-        coef = dot(charge_pad[1 + x, 1 + y], doubled, NT).astype(bf16)
-        coef_pad[2 + x, 2 + y] = coef
+        coef = dot(charge_v[x, y], doubled, NT).astype(bf16)
+        coef_v[x, y] = coef
+        coef_pad[(2 + x) * (ly + 4) + 2 + y] = coef
+        charge_pad[(1 + x) * (ly + 2) + 1 + y] = charge_v[x, y]
         cluster += dot(coef[:, :rank], transfer_v[x, y], NT)
     own = ct_v[...]
     term_v[0] = dot(cluster.astype(bf16), jnp.concatenate([own, own], axis=0), NT).astype(bf16)
 
+    near_start(0, 2 * INNER)
+    loads[8].start()
     pl.semaphore_wait(barrier, len(plane) + len(line) + len(around))
 
     def remote(source, target, send, recv, peer):
@@ -174,10 +191,10 @@
         view = buffer.at[pl.ds(1, buffer.shape[0] - 1)]
         pltpu.make_async_copy(view, view, sem).wait()
 
-    for step, peer in enumerate(plane, 1):
+    for step, peer in zip(plane_steps, plane):
         remote(term_v.at[0], term_v.at[step], stage_send.at[0], stage_recv.at[0], peer).start()
 
-    charge_copies, coef_copies, landed = [], [], []
+    charge_copies, coef_copies, landed, coef_landed = [], [], [], []
     for number, (sx, sy) in enumerate(SIDES):
         at_x, many_x, to_x = strip(sx, 1, lx)
         at_y, many_y, to_y = strip(sy, 1, ly)
@@ -185,7 +202,7 @@
         landed.append((land, many_x, many_y, to_x, to_y))
         charge_copies.append(
             remote(
-                charge_pad.at[pl.ds(1 + at_x, many_x), pl.ds(1 + at_y, many_y)],
+                charge_v.at[pl.ds(at_x, many_x), pl.ds(at_y, many_y)],
                 land,
                 charge_send.at[number],
                 charge_recv.at[number],
@@ -194,10 +211,12 @@
         )
         at_x, many_x, to_x = strip(sx, 2, lx)
         at_y, many_y, to_y = strip(sy, 2, ly)
+        land = coef_x.at[number] if number < 2 else coef_y.at[number - 2] if number < 4 else coef_corner.at[number - 4]
+        coef_landed.append((land, many_x, many_y, to_x, to_y))
         coef_copies.append(
             remote(
-                coef_pad.at[pl.ds(2 + at_x, many_x), pl.ds(2 + at_y, many_y)],
-                coef_pad.at[pl.ds(to_x, many_x), pl.ds(to_y, many_y)],
+                coef_v.at[pl.ds(at_x, many_x), pl.ds(at_y, many_y)],
+                land,
                 coef_send.at[number],
                 coef_recv.at[number],
                 beside(sx, sy),
@@ -206,8 +225,6 @@
     for copy in charge_copies + coef_copies:
         copy.start()
 
-    near_start(0, 2 * INNER)
-    loads[8].start()
     near_start(2 * INNER, 8)
     loads[9].start()
     for load in loads[4:8]:
@@ -217,21 +234,36 @@
         for y in range(ly):
             down = dot(own, transfer_v[x, y], NN).astype(bf16)
             fold_v[x, y] = dot(down, basis_v[x, y], NN).astype(bf16)
+            for entry in range(near_s.shape[2]):
+                place = near_s[x, y, entry]
+                near_at[x, y, entry] = x * (ly + 2) + y + place + (ly - 1) * lax.shift_right_logical(place * 11, 5)
+            for entry in range(far_s.shape[2]):
+                place = far_s[x, y, entry]
+                offset = jnp.minimum(jnp.maximum(place - 18, 4 * place - 30), place + 3)
+                far_at[x, y, entry] = (x + 2) * (ly + 4) + y + 2 + offset
         return carry
 
     lax.fori_loop(0, lx, fold, 0)
+
+    half = (lax.broadcasted_iota(jnp.int32, (1, 2 * rank), 1) >= rank).astype(jnp.int32)
+    loads[8].wait()
+    for step in range(n_line):
+        group = group_of(line_peer(step))
+        for pair in range(weight_v.shape[0] // 2):
+            kept = jnp.where(half == 0, pattern_s[group, 2 * pair], pattern_s[group, 2 * pair + 1]).astype(f32).astype(bf16)
+            columns = slice(2 * rank * pair, 2 * rank * (pair + 1))
+            allowed_v[step, :, columns] = weight_v[group, :, columns] * kept
+    part_v[...] = jnp.zeros_like(part_v)
 
     def take(number):
         charge_copies[number].wait_recv()
         land, many_x, many_y, to_x, to_y = landed[number]
         for x in range(many_x):
             for y in range(many_y):
-                charge_pad[to_x + x, to_y + y] = land[x, y]
+                charge_pad[(to_x + x) * (ly + 2) + to_y + y] = land[x, y]
 
     def coarse():
-        loads[8].wait()
         all_of(term_v, stage_recv.at[0])
-        half = (lax.broadcasted_iota(jnp.int32, (1, 2 * rank), 1) >= rank).astype(jnp.int32)
         terms = [term_v[step].astype(f32) for step in range(n_plane)]
         groups = [group_of(plane_peer(-step)) for step in range(n_plane)]
         sums = []
@@ -239,39 +271,29 @@
             total = jnp.zeros((vectors, 2 * rank), f32)
             for step in range(n_plane):
                 total += jnp.where(half == groups[step] - 2 * pair, terms[step], 0.0)
-            sums.append(total)
-        for step in range(n_line):
-            group = group_of(line_peer(step))
-            allowed = []
-            for pair, total in enumerate(sums):
-                kept = jnp.where(half == 0, pattern_s[group, 2 * pair], pattern_s[group, 2 * pair + 1]) != 0
-                allowed.append(jnp.where(kept, total, 0.0).astype(bf16))
-            part = dot(jnp.concatenate(allowed, axis=1), weight_v[group], NT)
-            part = jnp.concatenate([part, jnp.zeros_like(part)], axis=1)
-            if step == 0:
-                far_v[0] = part
-            else:
-                part_v[step] = part
-        for step, peer in enumerate(line, 1):
+            sums.append(total.astype(bf16))
+        parts = dot(jnp.concatenate(sums, axis=1), allowed_v[...].reshape(n_line * rank, -1), NT).astype(bf16)
+        far_v[0, :, :rank] = parts[:, :rank]
+        for step in range(1, n_line):
+            part_v[step, :, :rank] = parts[:, step * rank : (step + 1) * rank]
+        for step, peer in zip(line_steps, line):
             remote(part_v.at[step], far_v.at[step], stage_send.at[1], stage_recv.at[1], peer).start()
 
     def near_leaf(slot, x, y):
         total = jnp.zeros((vectors, points), f32)
         for entry in range(near_v.shape[1]):
-            place = near_s[x, y, entry]
-            down = lax.shift_right_logical(place * 11, 5)
-            total += dot(charge_pad[x + down, y + place - 3 * down], near_v[slot, entry], NT)
+            total += dot(charge_pad[near_at[x, y, entry]], near_v[slot, entry], NT)
         total_v[x, y] = total
 
     def near(step, carry):
+        @pl.when(step == 1)
+        def _():
+            near_start(8, len(order))
+
         for number in range(len(SIDES) // 2):
             pl.when(step == INNER + number)(functools.partial(take, number))
 
         pl.when(step == COARSE_AT)(coarse)
-
-        @pl.when(step == INNER)
-        def _():
-            near_start(8, len(order))
 
         slots = [2 * step + h for h in range(2)]
         for slot in slots:
@@ -285,24 +307,29 @@
         take(number)
 
     loads[9].wait()
-    for copy in coef_copies:
+    for copy, (land, many_x, many_y, to_x, to_y) in zip(coef_copies, coef_landed):
         copy.wait_recv()
-    left = lax.broadcasted_iota(jnp.int32, (vectors, 2 * rank), 1) < rank
-
-    def couple(x, carry):
+        for x in range(many_x):
+            for y in range(many_y):
+                coef_pad[(to_x + x) * (ly + 4) + to_y + y] = land[x, y]
+    in_left = (lax.broadcasted_iota(jnp.int32, (vectors, 2 * rank), 1) < rank).astype(f32).astype(bf16)
+    in_right = 1 - in_left
+
+    shape = (ly * vectors, ly * rank)
+    on_diagonal = lax.broadcasted_iota(jnp.int32, shape, 0) // vectors == lax.broadcasted_iota(jnp.int32, shape, 1) // rank
+
+    def to_points(values, matrices):
+        kept = jnp.where(on_diagonal, values, 0.0).astype(bf16)
+        return dot(kept, matrices.reshape(ly * rank, points), NN).reshape(ly, vectors, points)
+
+    def couple(x):
+        rows = []
         for y in range(ly):
-            picked = []
-            for entry in range(far_s.shape[2]):
-                place = far_s[x, y, entry]
-                offset = jnp.minimum(jnp.maximum(place - 18, 4 * place - 30), place + 3) + 18
-                down = lax.shift_right_logical(offset, 3)
-                picked.append(coef_pad[x + down, y + offset - 8 * down].astype(f32))
-            chosen = [
-                jnp.where(left, picked[2 * pair], picked[2 * pair + 1]).astype(bf16) for pair in range(len(picked) // 2)
-            ]
-            coupled = dot(jnp.concatenate(chosen, axis=1), coupling_v[x, y], NT).astype(bf16)
-            total_v[x, y] += dot(coupled, basis_v[x, y], NN)
-        return carry
+            picked = [coef_pad[far_at[x, y, entry]] for entry in range(far_s.shape[2])]
+            chosen = [picked[2 * pair] * in_left + picked[2 * pair + 1] * in_right for pair in range(len(picked) // 2)]
+            rows.append(jnp.concatenate(chosen, axis=1))
+        coupled = dot(jnp.concatenate(rows, axis=0), coupling_v[x].reshape(ly * rank, -1), NT)
+        total_v[x] += to_points(coupled, basis_v[x])
 
     corner_slots = range(2 * len(PAIRS) - 4, 2 * len(PAIRS))
     for slot in corner_slots:
@@ -310,15 +337,16 @@
     for slot in corner_slots:
         near_leaf(slot, *order[slot])
     for x in range(lx):
-        couple(x, 0)
+        couple(x)
 
     all_of(far_v, stage_recv.at[1])
-    far = far_v[0]
+    far = far_v[0].astype(f32)
     for step in range(1, n_line):
-        far += far_v[step]
-    far = far[:, :rank].astype(bf16)
-    for x, y in leaves:
-        out[x, y] = (total_v[x, y] + dot(far, fold_v[x, y], NN)).astype(bf16)
+        far += far_v[step].astype(f32)
+    far = jnp.concatenate([far[:, :rank]] * ly, axis=1)
+    far = jnp.concatenate([far] * ly, axis=0)
+    for x in range(lx):
+        out[x] = (total_v[x] + to_points(far, fold_v[x])).astype(bf16)
 
     all_of(term_v, stage_send.at[0])
     all_of(part_v, stage_send.at[1])
@@ -334,12 +362,15 @@
     n_plane, n_line = n_gy // SPLIT * SPLIT, n_gx // SPLIT * SPLIT
     sides = len(SIDES)
     scratch = [
-        pltpu.VMEM((lx + 2, ly + 2, vectors, points), bf16),
+        pltpu.VMEM(charges.shape, bf16),
+        pltpu.VMEM(((lx + 2) * (ly + 2), vectors, points), bf16),
         pltpu.VMEM((2, 1, ly, vectors, points), bf16),
         pltpu.VMEM((2, lx, 1, vectors, points), bf16),
         pltpu.VMEM((4, 1, 1, vectors, points), bf16),
         pltpu.VMEM(basis.shape, bf16),
         pltpu.VMEM((lx * ly,) + near_blocks.shape[2:], bf16),
+        pltpu.SMEM(near_list.shape, jnp.int32),
+        pltpu.SMEM(far_list.shape, jnp.int32),
         pltpu.SMEM(near_list.shape, jnp.int32),
         pltpu.SMEM(far_list.shape, jnp.int32),
         pltpu.VMEM(coupling.shape, bf16),
@@ -348,12 +379,17 @@
         pltpu.SMEM(coarse_group.shape, jnp.int32),
         pltpu.SMEM(coarse_pattern.shape, jnp.int32),
         pltpu.VMEM(coarse_coupling.shape, bf16),
-        pltpu.VMEM((lx + 4, ly + 4, vectors, halves), bf16),
+        pltpu.VMEM((n_line,) + coarse_coupling.shape[1:], bf16),
+        pltpu.VMEM((lx, ly, vectors, halves), bf16),
+        pltpu.VMEM(((lx + 4) * (ly + 4), vectors, halves), bf16),
+        pltpu.VMEM((2, 2, ly, vectors, halves), bf16),
+        pltpu.VMEM((2, lx, 2, vectors, halves), bf16),
+        pltpu.VMEM((4, 2, 2, vectors, halves), bf16),
         pltpu.VMEM(basis.shape, bf16),
         pltpu.VMEM((lx, ly, vectors, points), f32),
         pltpu.VMEM((n_plane, vectors, halves), bf16),
-        pltpu.VMEM((n_line, vectors, halves), f32),
-        pltpu.VMEM((n_line, vectors, halves), f32),
+        pltpu.VMEM((n_line, vectors, halves), bf16),
+        pltpu.VMEM((n_line, vectors, halves), bf16),
         pltpu.SemaphoreType.DMA((10,)),
         pltpu.SemaphoreType.DMA((lx * ly,)),
         pltpu.SemaphoreType.DMA((sides,)),

time: 20.1 us -> 19 us (0.945)
  Pallas kernels: 19.1 us -> 18.2 us
    pallas_call x1, Pallas kernels: 19.1 us -> 18.2 us  [local(): pl.pallas_call(functools.partial(kernel, n_gx, n_gy), out_shape=pltpu.VME...]
where the time goes in v3:
time: 19 us; the launch traced here: 18.9 us
  Pallas kernels  18.2 us (96%)
  local copies, waits for them, and re-layouts  0.66 us (3%)
    pallas_call x1, Pallas kernels, local(): pl.pallas_call(functools.partial(kernel, n_gx, n_gy), out_shape=pltpu.VME...  18.2 us
    unnamed x1, local copies, waits for them, and re-layouts  0.66 us

profile of v3, /device:TPU:1, one launch (start us, length us, event | category | flops | bytes accessed | tf_op | source)
XLA Modules:
  0.0 18.9 jit_solution(17227522458668433380)
XLA Ops:
  0.0 18.2 %shard_map.109 = bf16[4,4,16,256]{3,2,1,0:T(8,128)(2,1)S(1)} custom-call(bf16[4,4,16,256]{3,2,1,0:T(8,128)(2,1)} %charges.1, bf16[4,4,64,256]{3,2,1,0:T(8,128)(2,1)} %basis.1, bf16[4,4,8,256,256]{4,3,2,1,0:T(8,128)(2,1)} %near_blocks.1, s32[4,4,8]{2,1,0:T(4,128)} %near_list.1, s32[4,4,8]{2,1,0:T(4,128)} %far_list.1, bf16[4,4,64,512]{3,2,1,0:T(8,128)(2,1)} %coupling.1, ...), custom_call_target="tpu_custom_call" | custom-call | tf_op jit(solution)/shard_map/pallas_call | solution.py:402
  18.2 0.7 %copy.13 = bf16[4,4,16,256]{3,2,1,0:T(8,128)(2,1)} copy(bf16[4,4,16,256]{3,2,1,0:T(8,128)(2,1)S(1)} %shard_map.109) | data formatting | bytes 262144

commit v4 on v3

--- a/solution.py
+++ b/solution.py
@@ -168,9 +168,14 @@
     for load in loads[:4]:
         load.wait()
     cluster = jnp.zeros((vectors, rank), f32)
+    in_low = lax.broadcasted_iota(jnp.int32, (vectors, 2 * rank), 1) < rank
     for x, y in leaves:
-        doubled = jnp.concatenate([basis_v[x, y], basis_v[x, y]], axis=0)
-        coef = dot(charge_v[x, y], doubled, NT).astype(bf16)
+        if y == 0:
+            row = dot(charge_v[x].reshape(ly * vectors, points), basis_v[x].reshape(ly * rank, points), NT)
+        both = row[y * vectors : (y + 1) * vectors, y // 2 * 2 * rank : (y // 2 + 1) * 2 * rank]
+        swapped = jnp.concatenate([both[:, rank:], both[:, :rank]], axis=1)
+        coef = jnp.where(in_low, swapped, both) if y % 2 else jnp.where(in_low, both, swapped)
+        coef = coef.astype(bf16)
         coef_v[x, y] = coef
         coef_pad[(2 + x) * (ly + 4) + 2 + y] = coef
         charge_pad[(1 + x) * (ly + 2) + 1 + y] = charge_v[x, y]
@@ -178,8 +183,8 @@
     own = ct_v[...]
     term_v[0] = dot(cluster.astype(bf16), jnp.concatenate([own, own], axis=0), NT).astype(bf16)
 
+    loads[8].start()
     near_start(0, 2 * INNER)
-    loads[8].start()
     pl.semaphore_wait(barrier, len(plane) + len(line) + len(around))
 
     def remote(source, target, send, recv, peer):

time: 19 us -> 19 us (level)
  no operation moved by 1% of the time
where the time goes in v4:
time: 19 us; the launch traced here: 18.9 us
  Pallas kernels  18.2 us (96%)
  local copies, waits for them, and re-layouts  0.66 us (3%)
    pallas_call x1, Pallas kernels, local(): pl.pallas_call(functools.partial(kernel, n_gx, n_gy), out_shape=pltpu.VME...  18.2 us
    unnamed x1, local copies, waits for them, and re-layouts  0.66 us

profile of v4, /device:TPU:1, one launch (start us, length us, event | category | flops | bytes accessed | tf_op | source)
XLA Modules:
  0.0 18.9 jit_solution(6499921872777610741)
XLA Ops:
  0.0 18.2 %shard_map.109 = bf16[4,4,16,256]{3,2,1,0:T(8,128)(2,1)S(1)} custom-call(bf16[4,4,16,256]{3,2,1,0:T(8,128)(2,1)} %charges.1, bf16[4,4,64,256]{3,2,1,0:T(8,128)(2,1)} %basis.1, bf16[4,4,8,256,256]{4,3,2,1,0:T(8,128)(2,1)} %near_blocks.1, s32[4,4,8]{2,1,0:T(4,128)} %near_list.1, s32[4,4,8]{2,1,0:T(4,128)} %far_list.1, bf16[4,4,64,512]{3,2,1,0:T(8,128)(2,1)} %coupling.1, ...), custom_call_target="tpu_custom_call" | custom-call | tf_op jit(solution)/shard_map/pallas_call | solution.py:407
  18.2 0.7 %copy.13 = bf16[4,4,16,256]{3,2,1,0:T(8,128)(2,1)} copy(bf16[4,4,16,256]{3,2,1,0:T(8,128)(2,1)S(1)} %shard_map.109) | data formatting | bytes 262144
